TPU v7x, 256 devices: a whole 4x4x8 slice. The times are simulated.
256 devices in a mesh: dp: 8 (over y, x_lo), ctx: 32 (over z, x_hi, core).
Axes of the slice: x: 4 (x_hi: 2, x_lo: 2; x = x_hi * 2 + x_lo), y: 4, z: 8, core: 2. Of those that a mesh axis runs over, the one named last changes fastest.
Arguments:
- queries: bfloat16 [8, 4096, 768], P('dp', 'ctx'), may hold values from -12 to 12
- attn_keys: bfloat16 [8, 4096, 768], P('dp', 'ctx'), may hold values from -6 to 6
- attn_values: bfloat16 [8, 4096, 768], P('dp', 'ctx'), may hold values from -6 to 6
- residual: bfloat16 [8, 4096, 1536], P('dp', 'ctx'), may hold values from -10 to 10
- out_weight: bfloat16 [768, 1536], P('dp'), may hold values from -0.21875 to 0.21875
- conv_taps: float32 [31, 1536], replicated, may hold values from -1 to 1
- norm_gain: float32 [1536], replicated, may hold values from 0.5 to 2
- lengths: int32 [8], P('dp'), may hold values from 1024 to 4096, as said below
- cotangent: bfloat16 [8, 4096, 1536], P('dp', 'ctx'), may hold values from -7 to 7
Outputs:
- layer_out: bfloat16 [8, 4096, 1536], P('dp', 'ctx')
- grad_queries: bfloat16 [8, 4096, 768], P('dp', 'ctx')
- grad_keys: bfloat16 [8, 4096, 768], P('dp', 'ctx')
- grad_values: bfloat16 [8, 4096, 768], P('dp', 'ctx')
- grad_residual: bfloat16 [8, 4096, 1536], P('dp', 'ctx')
- grad_weight: float32 [768, 1536], P('ctx', 'dp')
- grad_taps: float32 [31, 1536], replicated
- grad_gain: float32 [1536], replicated
Inputs may be any that keep to these rules, and one draw needn't show every extreme that they name: Frames from lengths[u] on are padding; in every draw some utterance is whole.
All inputs are finite; a program needn't handle non-finite values.
Results may differ from a plain program's by a relative error of at most 0.035.
Values may be sent and summed in bfloat16 or wider, within the bound.
No kernel may reach another device: no remote copies, remote signals or barrier semaphores. Data moves between devices by JAX's collectives and lax.ppermute only.
A program may use at most 128 MiB of HBM per device.

v0:
```python
import math

import jax
import jax.numpy as jnp
from jax import lax
from jax.sharding import PartitionSpec as P

HEADS = 12
HD = 64
KTAPS = 31
HW = 768


MASK_FILL = -1e30
NORM_EPSILON = 1e-05


def extended(block, sides, width):
    for axis, dim in sides:
        count = lax.axis_size(axis)
        forward = [(i, i + 1) for i in range(count - 1)]
        backward = [(target, source) for source, target in forward]
        low = lax.ppermute(
            lax.slice_in_dim(block, block.shape[dim] - width, None, axis=dim), axis, forward
        )
        high = lax.ppermute(lax.slice_in_dim(block, 0, width, axis=dim), axis, backward)
        block = jnp.concatenate([low, block, high], axis=dim)
    return block


def norm_part(mid_float, norm_gain, frame_valid):
    row_mean = jnp.mean(mid_float, axis=-1, keepdims=True)
    centred = mid_float - row_mean
    spread = jnp.mean(centred * centred, axis=-1, keepdims=True)
    return centred * lax.rsqrt(spread + NORM_EPSILON) * norm_gain * frame_valid


def depthwise(padded, conv_taps, frames):
    summed = jnp.zeros((padded.shape[0], frames, padded.shape[2]), jnp.float32)
    for offset in range(KTAPS):
        summed = summed + conv_taps[offset] * padded[:, offset : offset + frames].astype(
            jnp.float32
        )
    return summed


def tap_grads(padded, grad_conv, frames):
    rows_out = []
    for offset in range(KTAPS):
        window = padded[:, offset : offset + frames].astype(jnp.float32)
        rows_out.append(jnp.sum(grad_conv.astype(jnp.float32) * window, axis=(0, 1)))
    return jnp.stack(rows_out)


def pair_columns(block, column_first):
    sliced = lax.dynamic_slice_in_dim(block, column_first, 2 * HD, 1)
    return sliced.reshape(sliced.shape[0], 2, HD)


def pair_scores(query_pair, key_pair, key_valid):
    scores = jnp.einsum(
        "qhd,khd->hqk", query_pair, key_pair, preferred_element_type=jnp.float32
    ) * (1.0 / math.sqrt(HD))
    return jnp.where(key_valid[None, None, :], scores, MASK_FILL)


def pair_terms(query_pair, datt_pair, log_pair, delta_pair, key_pair, value_pair, key_valid):
    scores = pair_scores(query_pair, key_pair, key_valid)
    prob = jnp.exp(scores - log_pair.T[:, :, None])
    grad_prob = jnp.einsum(
        "qhd,khd->hqk", datt_pair, value_pair, preferred_element_type=jnp.float32
    )
    grad_score = (prob * (grad_prob - delta_pair.T[:, :, None])).astype(jnp.bfloat16)
    return (prob.astype(jnp.bfloat16), grad_score)


def shards(
    queries, attn_keys, attn_values, residual, out_weight, conv_taps, norm_gain, lengths, cotangent
):
    frames = queries.shape[1]
    half_span = (KTAPS - 1) // 2
    pair_width = 2 * HD
    pair_count = HEADS // 2
    inv_root = 1.0 / math.sqrt(HD)
    gathered_keys, gathered_values = (
        lax.all_gather(attn_keys, "ctx", axis=1, tiled=True),
        lax.all_gather(attn_values, "ctx", axis=1, tiled=True),
    )
    key_all = gathered_keys[0]
    value_all = gathered_values[0]
    total_len = key_all.shape[0]
    first_frame = lax.axis_index("ctx") * frames
    key_valid = jnp.arange(total_len, dtype=jnp.int32) < lengths[0]
    local_valid = first_frame + jnp.arange(frames, dtype=jnp.int32) < lengths[0]
    query_local = queries[0]

    def forward_pair(pair_index, buffers):
        att_buf, log_buf = buffers
        column_first = pair_index * pair_width
        scores = pair_scores(
            pair_columns(query_local, column_first), pair_columns(key_all, column_first), key_valid
        )
        row_max = jnp.max(scores, axis=2, keepdims=True)
        shifted = jnp.exp(scores - row_max)
        row_sum = jnp.sum(shifted, axis=2, keepdims=True)
        weights_bf = (shifted / row_sum).astype(jnp.bfloat16)
        att_pair = jnp.einsum(
            "hqk,khd->qhd",
            weights_bf,
            pair_columns(value_all, column_first),
            preferred_element_type=jnp.float32,
        )
        log_pair = (row_max + jnp.log(row_sum))[:, :, 0].T
        att_buf = lax.dynamic_update_slice_in_dim(
            att_buf, att_pair.reshape(frames, pair_width).astype(jnp.bfloat16), column_first, 1
        )
        log_buf = lax.dynamic_update_slice_in_dim(log_buf, log_pair, pair_index * 2, 1)
        return (att_buf, log_buf)

    attended, log_total = lax.fori_loop(
        0,
        pair_count,
        forward_pair,
        (jnp.zeros((frames, HW), jnp.bfloat16), jnp.zeros((frames, HEADS), jnp.float32)),
    )
    weight_all = lax.all_gather(out_weight, "dp", axis=0, tiled=True)
    projected = jnp.dot(attended, weight_all, preferred_element_type=jnp.float32)
    residual_mid = (residual[0].astype(jnp.float32) + projected).astype(jnp.bfloat16)
    mid_float = residual_mid.astype(jnp.float32)
    frame_valid = local_valid.astype(jnp.float32)[:, None]
    normed = norm_part(mid_float, norm_gain, frame_valid).astype(jnp.bfloat16)
    padded = extended(normed[None], (("ctx", 1),), half_span)
    conv_pre = depthwise(padded, conv_taps, frames)[0]
    gate_sig = jax.nn.sigmoid(conv_pre)
    layer_out = (mid_float + conv_pre * gate_sig).astype(jnp.bfloat16)
    grad_out = cotangent[0].astype(jnp.float32)
    grad_conv = (grad_out * gate_sig * (1.0 + conv_pre * (1.0 - gate_sig))).astype(jnp.bfloat16)
    local_taps = tap_grads(padded, grad_conv[None], frames)
    grad_padded = extended(grad_conv[None], (("ctx", 1),), half_span)
    grad_normed = depthwise(grad_padded, conv_taps[::-1], frames)[0]
    norm_value, norm_pull = jax.vjp(
        lambda mid_in, gain_in: norm_part(mid_in, gain_in, frame_valid), mid_float, norm_gain
    )
    norm_back, local_gain = norm_pull(grad_normed)
    grad_taps, grad_gain = lax.psum((local_taps, local_gain), ("dp", "ctx"))
    grad_residual = (grad_out + norm_back).astype(jnp.bfloat16)
    weight_part = lax.psum_scatter(
        lax.dot_general(
            attended, grad_residual, (((0,), (0,)), ((), ())), preferred_element_type=jnp.float32
        ).astype(jnp.bfloat16),
        "ctx",
        scatter_dimension=0,
        tiled=True,
    )
    grad_weight = lax.psum_scatter(weight_part, "dp", scatter_dimension=1, tiled=True).astype(
        jnp.float32
    )
    grad_att = lax.dot_general(
        grad_residual, weight_all, (((1,), (1,)), ((), ())), preferred_element_type=jnp.float32
    ).astype(jnp.bfloat16)
    row_delta = jnp.sum(
        (grad_att.astype(jnp.float32) * attended.astype(jnp.float32)).reshape(frames, HEADS, HD),
        axis=2,
    )

    def backward_pair(pair_index, buffers):
        query_buf, key_buf, value_buf = buffers
        column_first = pair_index * pair_width
        query_pair = pair_columns(query_local, column_first)
        datt_pair = pair_columns(grad_att, column_first)
        key_pair = pair_columns(key_all, column_first)
        value_pair = pair_columns(value_all, column_first)
        log_pair = lax.dynamic_slice_in_dim(log_total, pair_index * 2, 2, 1)
        delta_pair = lax.dynamic_slice_in_dim(row_delta, pair_index * 2, 2, 1)
        prob_bf, grad_score = pair_terms(
            query_pair, datt_pair, log_pair, delta_pair, key_pair, value_pair, key_valid
        )
        query_grad = (
            jnp.einsum("hqk,khd->qhd", grad_score, key_pair, preferred_element_type=jnp.float32)
            * inv_root
        )
        key_grad = (
            jnp.einsum("hqk,qhd->khd", grad_score, query_pair, preferred_element_type=jnp.float32)
            * inv_root
        ).astype(jnp.bfloat16)
        value_grad = jnp.einsum(
            "hqk,qhd->khd", prob_bf, datt_pair, preferred_element_type=jnp.float32
        ).astype(jnp.bfloat16)
        query_buf = lax.dynamic_update_slice_in_dim(
            query_buf, query_grad.reshape(frames, pair_width), column_first, 1
        )
        key_buf = lax.dynamic_update_slice_in_dim(
            key_buf, key_grad.reshape(total_len, pair_width), column_first, 1
        )
        value_buf = lax.dynamic_update_slice_in_dim(
            value_buf, value_grad.reshape(total_len, pair_width), column_first, 1
        )
        return (query_buf, key_buf, value_buf)

    start_bufs = (
        jnp.zeros((frames, HW), jnp.float32),
        jnp.zeros((total_len, HW), jnp.bfloat16),
        jnp.zeros((total_len, HW), jnp.bfloat16),
    )
    query_sum, key_terms, value_terms = lax.fori_loop(0, pair_count, backward_pair, start_bufs)
    key_sum, value_sum = (
        lax.psum_scatter(key_terms, "ctx", scatter_dimension=0, tiled=True).astype(jnp.float32),
        lax.psum_scatter(value_terms, "ctx", scatter_dimension=0, tiled=True).astype(jnp.float32),
    )
    return (
        layer_out[None],
        query_sum.astype(jnp.bfloat16)[None],
        key_sum.astype(jnp.bfloat16)[None],
        value_sum.astype(jnp.bfloat16)[None],
        grad_residual[None],
        grad_weight,
        grad_taps,
        grad_gain,
    )


def solution(mesh):
    placed = (
        P("dp", "ctx", None),
        P("dp", "ctx", None),
        P("dp", "ctx", None),
        P("dp", "ctx", None),
        P("dp", None),
        P(),
        P(),
        P("dp"),
        P("dp", "ctx", None),
    )
    return jax.shard_map(
        shards,
        mesh=mesh,
        in_specs=placed,
        out_specs=(
            P("dp", "ctx", None),
            P("dp", "ctx", None),
            P("dp", "ctx", None),
            P("dp", "ctx", None),
            P("dp", "ctx", None),
            P("ctx", "dp"),
            P(),
            P(),
        ),
        check_vma=False,
    )
```

profile of v0, /device:TPU:8, one launch (start us, length us, event | category | flops | bytes accessed | tf_op | source)
XLA Modules:
  0.0 1009.0 jit_solution(6546268065607728544)
XLA Ops:
  7.2 1.7 copy.36
  9.0 1.7 copy.34
  12.2 1.8 slice_reduce_fusion.30
  15.2 96.5 %all-gather.6.cloned.1.call-done = bf16[1,4096,768]{1,2,0:T(8,128)(2,1)} async-done(((bf16[1,128,768]{1,2,0:T(8,128)(2,1)}), bf16[1,4096,768]{1,2,0:T(8,128)(2,1)}) %all-gather.6.cloned.1.call-update) | async-done | bytes 6291472 | tf_op jit(solution)/shard_map/all_gather | solution.py:86
  111.7 97.3 %all-gather.4.cloned.1.call-done = bf16[1,4096,768]{1,2,0:T(8,128)(2,1)} async-done(((bf16[1,128,768]{1,2,0:T(8,128)(2,1)}), bf16[1,4096,768]{1,2,0:T(8,128)(2,1)}) %all-gather.4.cloned.1.call-update) | async-done | bytes 6291472 | tf_op jit(solution)/shard_map/all_gather | solution.py:87
  209.7 33.4 %while.34 = (s32[]{:T(128)}, bf16[128,768]{0,1:T(8,128)(2,1)S(1)}, f32[128,12]{0,1:T(8,128)}, bf16[4096,768]{0,1:T(8,128)(2,1)}, bf16[128,768]{0,1:T(8,128)(2,1)...) while((s32[]{:T(128)}, bf16[128,768]{0,1:T(8,128)(2,1)S(1)}, ...), condition=%wide.region_3.4_spmd.clone, body=%wide.region_0.3_spmd.clone.sunk | while | flops 276844288 | bytes 19087604 | solution.py:120
  210.4 1.7 constant_dynamic-slice_fusion.15
  216.0 1.7 constant_dynamic-slice_fusion.15
  221.5 1.7 constant_dynamic-slice_fusion.15
  227.1 1.7 constant_dynamic-slice_fusion.15
  232.6 1.7 constant_dynamic-slice_fusion.15
  238.2 1.7 constant_dynamic-slice_fusion.15
  243.1 22.1 %all-gather.8.cloned.1.call-done = bf16[768,1536]{1,0:T(8,128)(2,1)} async-done(((bf16[96,1536]{1,0:T(8,128)(2,1)}), bf16[768,1536]{1,0:T(8,128)(2,1)}) %all-gather.8.cloned.1.call-update) | async-done | bytes 2359312 | tf_op jit(solution)/shard_map/all_gather | solution.py:126
  265.2 2.2 fusion.174
  268.1 1.7 collective-permute-start
  271.1 1.4 slice_reduce_fusion.29
  272.5 2.9 collective-permute-done.1
  276.0 5.5 fusion.102
  281.6 6.3 collective-permute-start.2
  287.9 1.5 collective-permute-start.3
  289.4 1.6 collective-permute-done.3
  291.0 6.2 multiply_reduce_fusion
  297.3 1.5 fusion.47
  299.0 2.2 convolution_convert_fusion.1
  301.2 1.7 copy.37
  310.0 2.4 fusion.103
  317.7 2.5 fusion.88
  320.8 1.8 fusion.87
  331.0 98.0 %reduce-scatter.11.cloned.1.call-done = bf16[24,1536]{1,0:T(8,128)(2,1)} async-done(((bf16[768,1536]{1,0:T(8,128)(2,1)}), bf16[24,1536]{1,0:T(8,128)(2,1)}) %reduce-scatter.11.cloned.1.call-update) | async-done | bytes 73744 | tf_op jit(solution)/shard_map/reduce_scatter | solution.py:147
  429.0 1.8 copy.43
  430.9 2.5 convert_multiply_fusion.64
  433.6 5.9 stack.127
  439.9 3.0 broadcast.176.clone2
  442.9 3.0 broadcast.176.clone
  445.9 74.0 %while.35 = (s32[]{:T(128)}, bf16[128,768]{1,0:T(8,128)(2,1)S(1)}, bf16[4096,768]{1,0:T(8,128)(2,1)}, bf16[4096,768]{1,0:T(8,128)(2,1)}, bf16[4096,768]{0,1:T(8,...) while((s32[]{:T(128)}, bf16[128,768]{1,0:T(8,128)(2,1)S(1)}, ...), condition=%wide.region_10.11_spmd.clone, body=%wide.region_9.10_spmd.clone.sunk | while | flops 680038400 | bytes 37206308 | solution.py:205
  456.6 1.6 constant_dynamic-update-slice_fusion.12
  469.0 1.6 constant_dynamic-update-slice_fusion.12
  481.3 1.6 constant_dynamic-update-slice_fusion.12
  493.6 1.6 constant_dynamic-update-slice_fusion.12
  499.5 1.3 constant_dynamic-slice_fusion.17
  505.9 1.6 constant_dynamic-update-slice_fusion.12
  511.8 1.3 constant_dynamic-slice_fusion.17
  518.2 1.6 constant_dynamic-update-slice_fusion.12
  520.7 73.6 %psum.15 = f32[1536]{0:T(1024)} all-reduce(f32[1536]{0:T(1024)S(1)} %copy-done.11), channel_id=1, replica_groups=mesh['dp'=8,'ctx'=32] {'dp','ctx'}, use_global_device_ids=true, to_apply=%region_48.49 | all-reduce | flops 1536 | bytes 12288 | tf_op jit(solution)/shard_map/psum | solution.py:145
  595.8 124.5 %all-reduce.2.cloned.1.call-done = f32[31,1536]{1,0:T(8,128)} async-done(((f32[31,1536]{1,0:T(8,128)}), f32[31,1536]{1,0:T(8,128)}) %all-reduce.2.cloned.1.call-update) | async-done | bytes 190480 | tf_op jit(solution)/shard_map/psum | solution.py:145
  720.3 140.5 %reduce-scatter.9.cloned.1.call-done = bf16[128,768]{1,0:T(8,128)(2,1)} async-done(((bf16[4096,768]{1,0:T(8,128)(2,1)}), bf16[128,768]{1,0:T(8,128)(2,1)}) %reduce-scatter.9.cloned.1.call-update) | async-done | bytes 196624 | tf_op jit(solution)/shard_map/reduce_scatter | solution.py:208
  860.8 139.7 %reduce-scatter.7.cloned.1.call-done = bf16[128,768]{1,0:T(8,128)(2,1)} async-done(((bf16[4096,768]{1,0:T(8,128)(2,1)}), bf16[128,768]{1,0:T(8,128)(2,1)}) %reduce-scatter.7.cloned.1.call-update) | async-done | bytes 196624 | tf_op jit(solution)/shard_map/reduce_scatter | solution.py:207
  1000.6 1.6 copy.125
  (237 shorter events, 113.9 us)
Async XLA Ops:
  7.2 104.5 %all-gather.6.cloned.1.call-start = ((), (), s32[]{:S(2)}) async-start(), calls=%async_computation.5 | async-start | bytes 6488064 | tf_op jit(solution)/shard_map/all_gather | solution.py:86
  9.0 200.0 %all-gather.4.cloned.1.call-start = ((), (), s32[]{:S(2)}) async-start(), calls=%async_computation.4 | async-start | bytes 6488064 | tf_op jit(solution)/shard_map/all_gather | solution.py:87
  10.8 254.4 %all-gather.8.cloned.1.call-start = ((), (), s32[]{:S(2)}) async-start(), calls=%async_computation.6 | async-start | bytes 2654208 | tf_op jit(solution)/shard_map/all_gather | solution.py:126
  11.5 417.4 %reduce-scatter.11.cloned.1.call-start = ((), (), s32[]{:S(2)}) async-start(), calls=%async_computation.9 | async-start | bytes 2433024 | tf_op jit(solution)/shard_map/reduce_scatter | solution.py:147
  209.6 55.6 %copy-start.7 = (bf16[1,128,1536]{2,1,0:T(8,128)(2,1)S(1)}, bf16[1,128,1536]{2,1,0:T(8,128)(2,1)}, u32[]{:S(2)}) copy-start(bf16[1,128,1536]{2,1,0:T(8,128)(2,1)} %param.16) | copy-start | bytes 1179652
  243.1 24.6 %copy-start.3 = (bf16[128,768]{0,1:T(8,128)(2,1)}, bf16[128,768]{0,1:T(8,128)(2,1)S(1)}, u32[]{:S(2)}) copy-start(bf16[128,768]{0,1:T(8,128)(2,1)S(1)} %get-tuple-element.319) | copy-start | bytes 589828
  243.1 24.6 %copy-start.5 = (bf16[128,768]{0,1:T(8,128)(2,1)}, bf16[128,768]{0,1:T(8,128)(2,1)S(1)}, u32[]{:S(2)}) copy-start(bf16[128,768]{0,1:T(8,128)(2,1)S(1)} %get-tuple-element.762) | copy-start | bytes 589828
  243.1 24.6 %copy-start.10 = (f32[1536]{0:T(1024)S(1)}, f32[1536]{0:T(1024)}, u32[]{:S(2)}) copy-start(f32[1536]{0:T(1024)} %param.19) | copy-start | bytes 18436
  243.1 32.9 %copy-start.2 = (bf16[1,128,1536]{2,1,0:T(8,128)(2,1)S(1)}, bf16[1,128,1536]{2,1,0:T(8,128)(2,1)}, u32[]{:S(2)}) copy-start(bf16[1,128,1536]{2,1,0:T(8,128)(2,1)} %param.21) | copy-start | bytes 1179652
  268.1 4.4 collective-permute-start
  269.8 5.6 collective-permute-start.1
  272.5 2.9 copy-start.6
  275.4 0.6 copy-start.8
  281.6 17.4 %copy-start.4 = (bf16[128,768]{0,1:T(8,128)(2,1)S(1)}, bf16[128,768]{0,1:T(8,128)(2,1)}, u32[]{:S(2)}) copy-start(bf16[128,768]{0,1:T(8,128)(2,1)} %copy-done.3) | copy-start | bytes 589828
  281.6 7.8 collective-permute-start.2
  287.9 3.1 collective-permute-start.3
  299.0 131.9 %copy-start.1 = (bf16[128,1536]{1,0:T(8,128)(2,1)}, bf16[128,1536]{1,0:T(8,128)(2,1)S(1)}, u32[]{:S(2)}) copy-start(bf16[128,1536]{1,0:T(8,128)(2,1)S(1)} %fusion.53) | copy-start | bytes 1179652
  299.0 131.9 %copy-start = (bf16[768,1536]{1,0:T(8,128)(2,1)S(1)}, bf16[768,1536]{1,0:T(8,128)(2,1)}, u32[]{:S(2)}) copy-start(bf16[768,1536]{1,0:T(8,128)(2,1)} %all-gather.8.cloned.1.call-done) | copy-start | bytes 7077892
  301.2 293.1 %reduce-scatter.13.cloned.1.call-start = ((), (), s32[]{:S(2)}) async-start(), calls=%async_computation.11 | async-start | bytes 442368
  310.0 123.6 %copy-start.12 = (f32[1,1536]{1,0:T(1,128)S(1)}, f32[1,1536]{1,0:T(1,128)}, u32[]{:S(2)}) copy-start(f32[1,1536]{1,0:T(1,128)} %stack.125) | copy-start | bytes 18436
  430.8 289.5 %all-reduce.2.cloned.1.call-start = ((), (), s32[]{:S(2)}) async-start(), calls=%async_computation.10 | async-start | bytes 393216 | tf_op jit(solution)/shard_map/psum | solution.py:145
  439.6 421.3 %reduce-scatter.9.cloned.1.call-start = ((), (), s32[]{:S(2)}) async-start(), calls=%async_computation.8 | async-start | bytes 6488064 | tf_op jit(solution)/shard_map/reduce_scatter | solution.py:208
  519.8 0.8 copy-start.9
  519.9 0.8 copy-start.11
  519.9 480.7 %reduce-scatter.7.cloned.1.call-start = ((), (), s32[]{:S(2)}) async-start(), calls=%async_computation.7 | async-start | bytes 6488064 | tf_op jit(solution)/shard_map/reduce_scatter | solution.py:207
Sparse Core Ops, SparseCore 0:
  11.1 100.5 all-gather.5
  114.8 94.1 all-gather.3
  210.8 54.3 all-gather.7
  301.3 127.6 reduce-scatter.10
  431.5 36.0 reduce-scatter.12
  473.6 246.7 all-reduce.1
  725.2 135.6 reduce-scatter.8
  865.7 134.8 reduce-scatter.6
where the time goes:
time: 1010 us
  waiting for transfers between devices  725 us (72%)
  local copies, waits for them, and re-layouts  107 us (11%)
  blocking collectives  73.6 us (7%)
  matrix products  39.7 us (4%)
  other arithmetic  37 us (4%)
  between operations  15.1 us (1%)
  starting transfers between devices  11.3 us (1%)
    reduce_scatter x1, waiting for transfers between devices, shards(): lax.psum_scatter(value_terms, 'ctx', scatter_dimension=0, tiled=True)  141 us
    reduce_scatter x1, waiting for transfers between devices, shards(): lax.psum_scatter(key_terms, 'ctx', scatter_dimension=0, tiled=True)  140 us
    psum x1, waiting for transfers between devices, shards(): grad_taps, grad_gain = lax.psum((local_taps, local_gain), ('dp', 'ctx'))  125 us
    reduce_scatter x1, waiting for transfers between devices, shards(): lax.psum_scatter(lax.dot_general(attended, grad_residual, (((0,), (0,)),...  98 us
    all_gather x1, waiting for transfers between devices, shards(): lax.all_gather(attn_values, 'ctx', axis=1, tiled=True)  97.3 us
    all_gather x1, waiting for transfers between devices, shards(): lax.all_gather(attn_keys, 'ctx', axis=1, tiled=True)  96.5 us
    psum x1, blocking collectives, shards(): grad_taps, grad_gain = lax.psum((local_taps, local_gain), ('dp', 'ctx'))  73.6 us
    dynamic_slice x42, local copies, waits for them, and re-layouts, pair_columns(): sliced = lax.dynamic_slice_in_dim(block, column_first, 2 * HD, 1)  35.7 us
  transfers between devices with their start and end apart: 12, of which 9 were waited for; matrix products, arithmetic and copies ran while one was open for 16% of the time, Pallas kernels for 0%

commit v1 on v0

v1 whole, which is shorter than its diff:
```python
import math

import jax
import jax.numpy as jnp
from jax import lax
from jax.sharding import PartitionSpec as P

HEADS = 12
HD = 64
KTAPS = 31
HW = 768
GROUPS = 4
PER = 8
GH = HEADS // GROUPS
GW = GH * HD
HALO = 32
MASK_FILL = -1e30
NORM_EPSILON = 1e-05


def swap(block, axis, mask):
    count = lax.axis_size(axis)
    return lax.ppermute(block, axis, [(i, i ^ mask) for i in range(count)])


def bit_of(index, mask):
    return (index & mask) != 0


def by_group(blocks, group):
    first = bit_of(group, 1)
    second = bit_of(group, 2)
    low = [jnp.where(first, blocks[k ^ 1], blocks[k]) for k in range(GROUPS)]
    return [jnp.where(second, low[k ^ 2], low[k]) for k in range(GROUPS)]


def neighbours(block, width):
    count = lax.axis_size("ctx")
    forward = [(i, i + 1) for i in range(count - 1)]
    backward = [(target, source) for source, target in forward]
    low = lax.ppermute(block[block.shape[0] - width :], "ctx", forward)
    high = lax.ppermute(block[:width], "ctx", backward)
    return low, high


def norm_part(mid_float, norm_gain, frame_valid):
    row_mean = jnp.mean(mid_float, axis=-1, keepdims=True)
    centred = mid_float - row_mean
    spread = jnp.mean(centred * centred, axis=-1, keepdims=True)
    return centred * lax.rsqrt(spread + NORM_EPSILON) * norm_gain * frame_valid


def depthwise(padded, conv_taps, frames, start):
    summed = jnp.zeros((frames, padded.shape[1]), jnp.float32)
    for offset in range(KTAPS):
        summed = summed + conv_taps[offset] * padded[
            start + offset : start + offset + frames
        ].astype(jnp.float32)
    return summed


def tap_grads(padded, grad_conv, frames, start):
    rows_out = []
    for offset in range(KTAPS):
        window = padded[start + offset : start + offset + frames].astype(jnp.float32)
        rows_out.append(jnp.sum(grad_conv.astype(jnp.float32) * window, axis=0))
    return rows_out


def attention(query, pairs, bias):
    outs, logs = [], []
    for h in range(GH):
        q = query[:, h * 128 : h * 128 + HD]
        k = pairs[:, h * 128 : h * 128 + HD]
        v = pairs[:, h * 128 + HD : (h + 1) * 128]
        scores = (
            lax.dot_general(q, k, (((1,), (1,)), ((), ())), preferred_element_type=jnp.float32)
            + bias
        )
        row_max = jnp.max(scores, axis=1, keepdims=True)
        shifted = jnp.exp(scores - row_max)
        row_sum = jnp.sum(shifted, axis=1, keepdims=True)
        weights = (shifted / row_sum).astype(jnp.bfloat16)
        outs.append(jnp.dot(weights, v, preferred_element_type=jnp.float32).astype(jnp.bfloat16))
        logs.append(row_max + jnp.log(row_sum))
    return jnp.concatenate(outs, axis=1), jnp.concatenate(logs, axis=1)


def attention_back(query, pairs, bias, logs, datt, delta):
    query_grads, pair_grads = [], []
    for h in range(GH):
        q = query[:, h * 128 : h * 128 + HD]
        k = pairs[:, h * 128 : h * 128 + HD]
        v = pairs[:, h * 128 + HD : (h + 1) * 128]
        d = datt[:, h * HD : (h + 1) * HD]
        scores = (
            lax.dot_general(q, k, (((1,), (1,)), ((), ())), preferred_element_type=jnp.float32)
            + bias
        )
        prob = jnp.exp(scores - logs[:, h : h + 1])
        grad_prob = lax.dot_general(
            d, v, (((1,), (1,)), ((), ())), preferred_element_type=jnp.float32
        )
        grad_score = (prob * (grad_prob - delta[:, h : h + 1])).astype(jnp.bfloat16)
        query_grads.append(
            (jnp.dot(grad_score, k, preferred_element_type=jnp.float32) * (1.0 / 8.0)).astype(
                jnp.bfloat16
            )
        )
        contract = (((0,), (0,)), ((), ()))
        pair_grads.append(
            lax.dot_general(grad_score, q, contract, preferred_element_type=jnp.float32).astype(
                jnp.bfloat16
            )
        )
        pair_grads.append(
            lax.dot_general(
                prob.astype(jnp.bfloat16), d, contract, preferred_element_type=jnp.float32
            ).astype(jnp.bfloat16)
        )
    return jnp.concatenate(query_grads, axis=1), jnp.concatenate(pair_grads, axis=1)


def add(first, second):
    return (first.astype(jnp.float32) + second.astype(jnp.float32)).astype(first.dtype)


def halve(block, dim, axis, mask, index):
    mine = (index & mask) // mask
    kept = lax.dynamic_index_in_dim(block, mine, dim, keepdims=False)
    sent = lax.dynamic_index_in_dim(block, 1 - mine, dim, keepdims=False)
    return add(kept, swap(sent, axis, mask))


def regather(block, axis, mask, index):
    other = swap(block, axis, mask)
    high = bit_of(index, mask)
    return jnp.concatenate(
        [jnp.where(high, other, block), jnp.where(high, block, other)], axis=0
    )


def sum_everywhere(rows, ctx, dp):
    part = rows
    for mask in (1, 2, 4):
        part = part.reshape(2, part.shape[0] // 2, part.shape[1])
        part = halve(part, 0, "ctx", mask, ctx)
    for mask in (8, 16):
        part = part + swap(part, "ctx", mask)
    mask = 1
    while mask < lax.axis_size("dp"):
        part = part + swap(part, "dp", mask)
        mask *= 2
    for mask in (4, 2, 1):
        part = regather(part, "ctx", mask, ctx)
    return part


def shards(
    queries, attn_keys, attn_values, residual, out_weight, conv_taps, norm_gain, lengths, cotangent
):
    frames = queries.shape[1]
    width = residual.shape[2]
    ctx = lax.axis_index("ctx")
    dp = lax.axis_index("dp")
    dp_size = lax.axis_size("dp")
    group = ctx // PER
    member = ctx % PER
    length = lengths[0]

    weight_all = lax.all_gather(out_weight, "dp", axis=0, tiled=True)
    cot_low, cot_high = neighbours(cotangent[0], HALO // 2)

    query_scaled = (queries[0].astype(jnp.float32) * (1.0 / math.sqrt(HD))).astype(jnp.bfloat16)
    pieces = []
    for g in range(GROUPS):
        cols = []
        for h in range(GH):
            first = (g * GH + h) * HD
            cols += [attn_keys[0][:, first : first + HD], attn_values[0][:, first : first + HD]]
        cols.append(query_scaled[:, g * GW : (g + 1) * GW])
        pieces.append(jnp.concatenate(cols, axis=1))
    relative = by_group(pieces, group)
    received = [relative[0]] + [swap(relative[k], "ctx", k * PER) for k in range(1, GROUPS)]
    held = jnp.concatenate(by_group(received, group), axis=0)
    own_pairs, query = held[:, : GH * 128], held[:, GH * 128 :]
    rows = own_pairs.shape[0]
    query = jnp.pad(query.reshape(rows, GH, HD), ((0, 0), (0, 0), (0, HD))).reshape(rows, GH * 128)

    half = rows // 2
    from_x = swap(own_pairs, "ctx", 2)
    from_z = swap(own_pairs, "ctx", 4)
    diag = jnp.concatenate(
        [swap(from_z[:half], "ctx", 2), swap(from_x[half:], "ctx", 4)], axis=0
    )
    near = jnp.concatenate([own_pairs, from_x, from_z, diag], axis=0)
    pairs = jnp.concatenate([near, swap(near, "ctx", 1)], axis=0)
    order = [0, 2, 4, 6, 1, 3, 5, 7]
    starts = jnp.concatenate(
        [
            jnp.stack([(PER * g + (member ^ k)) * frames for g in range(GROUPS)])
            for k in order
        ]
    )
    positions = (starts[:, None] + jnp.arange(frames, dtype=jnp.int32)[None, :]).reshape(1, -1)
    bias = jnp.where(positions < length, 0.0, MASK_FILL).astype(jnp.float32)

    att_heads, log_total = attention(query, pairs, bias)

    def rows_home(block):
        parts = by_group([block[g * frames : (g + 1) * frames] for g in range(GROUPS)], group)
        back = [parts[0]] + [swap(parts[k], "ctx", k * PER) for k in range(1, GROUPS)]
        return by_group(back, group)

    attended = jnp.concatenate(rows_home(att_heads), axis=1)
    projected = jnp.dot(attended, weight_all, preferred_element_type=jnp.float32)
    residual_mid = (residual[0].astype(jnp.float32) + projected).astype(jnp.bfloat16)
    mid_float = residual_mid.astype(jnp.float32)
    first_frame = ctx * frames
    local_valid = first_frame + jnp.arange(frames, dtype=jnp.int32) < length
    frame_valid = local_valid.astype(jnp.float32)[:, None]
    normed = norm_part(mid_float, norm_gain, frame_valid).astype(jnp.bfloat16)
    norm_low, norm_high = neighbours(normed, HALO)
    padded = jnp.concatenate([norm_low, normed, norm_high], axis=0)
    side = HALO // 2
    cot_ext = jnp.concatenate([cot_low, cotangent[0], cot_high], axis=0).astype(jnp.float32)
    conv_ext = depthwise(padded, conv_taps, frames + HALO, 1)
    sig_ext = jax.nn.sigmoid(conv_ext)
    grad_conv_ext = (cot_ext * sig_ext * (1.0 + conv_ext * (1.0 - sig_ext))).astype(jnp.bfloat16)
    conv_pre = conv_ext[side : side + frames]
    gate_sig = sig_ext[side : side + frames]
    layer_out = (mid_float + conv_pre * gate_sig).astype(jnp.bfloat16)
    grad_out = cotangent[0].astype(jnp.float32)
    local_taps = tap_grads(padded, grad_conv_ext[side : side + frames], frames, side + 1)
    grad_normed = depthwise(grad_conv_ext, conv_taps[::-1], frames, 1)
    norm_value, norm_pull = jax.vjp(
        lambda mid_in, gain_in: norm_part(mid_in, gain_in, frame_valid), mid_float, norm_gain
    )
    norm_back, local_gain = norm_pull(grad_normed)
    summed = sum_everywhere(jnp.stack(local_taps + [local_gain]), ctx, dp)
    grad_taps, grad_gain = summed[:KTAPS], summed[KTAPS]
    grad_residual = (grad_out + norm_back).astype(jnp.bfloat16)

    grad_att = lax.dot_general(
        grad_residual, weight_all, (((1,), (1,)), ((), ())), preferred_element_type=jnp.float32
    ).astype(jnp.bfloat16)

    parts = by_group([grad_att[:, g * GW : (g + 1) * GW] for g in range(GROUPS)], group)
    arrived = [parts[0]] + [swap(parts[k], "ctx", k * PER) for k in range(1, GROUPS)]
    datt = jnp.concatenate(by_group(arrived, group), axis=0)
    delta = jnp.sum(
        (datt.astype(jnp.float32) * att_heads.astype(jnp.float32)).reshape(rows, GH, HD), axis=2
    )

    part = lax.dot_general(
        attended, grad_residual, (((0,), (0,)), ((), ())), preferred_element_type=jnp.float32
    ).astype(jnp.bfloat16)
    part = part.reshape(2, 2, 2, 2, 2, HW // 32, width)
    part = halve(part, 4, "ctx", 1, ctx)
    part = halve(part, 3, "ctx", 2, ctx)
    part = halve(part, 2, "ctx", 4, ctx)
    part = halve(part, 1, "ctx", 8, ctx)
    part = halve(part, 0, "ctx", 16, ctx)
    mask = dp_size // 2
    while mask:
        part = part.reshape(part.shape[0], 2, part.shape[1] // 2)
        part = halve(part, 1, "dp", mask, dp)
        mask //= 2
    grad_weight = part.astype(jnp.float32)

    query_grad, pair_grad = attention_back(query, pairs, bias, log_total, datt, delta)

    total = pair_grad.shape[0]
    near = add(pair_grad[: total // 2], swap(pair_grad[total // 2 :], "ctx", 1))
    own, to_x, to_z, far = [near[i * rows : (i + 1) * rows] for i in range(4)]
    far_x = swap(far[:half], "ctx", 2)
    far_z = swap(far[half:], "ctx", 4)
    to_z = jnp.concatenate([add(to_z[:half], far_x), to_z[half:]], axis=0)
    to_x = jnp.concatenate([to_x[:half], add(to_x[half:], far_z)], axis=0)
    pair_sum = (
        own.astype(jnp.float32)
        + swap(to_x, "ctx", 2).astype(jnp.float32)
        + swap(to_z, "ctx", 4).astype(jnp.float32)
    ).astype(jnp.bfloat16)
    home = rows_home(jnp.concatenate([pair_sum, query_grad], axis=1))
    keys_out, values_out, queries_out = [], [], []
    for block in home:
        for h in range(GH):
            keys_out.append(block[:, h * 128 : h * 128 + HD])
            values_out.append(block[:, h * 128 + HD : (h + 1) * 128])
        queries_out.append(block[:, GH * 128 :])
    return (
        layer_out[None],
        jnp.concatenate(queries_out, axis=1)[None],
        jnp.concatenate(keys_out, axis=1)[None],
        jnp.concatenate(values_out, axis=1)[None],
        grad_residual[None],
        grad_weight,
        grad_taps,
        grad_gain,
    )


def solution(mesh):
    placed = (
        P("dp", "ctx", None),
        P("dp", "ctx", None),
        P("dp", "ctx", None),
        P("dp", "ctx", None),
        P("dp", None),
        P(),
        P(),
        P("dp"),
        P("dp", "ctx", None),
    )
    return jax.shard_map(
        shards,
        mesh=mesh,
        in_specs=placed,
        out_specs=(
            P("dp", "ctx", None),
            P("dp", "ctx", None),
            P("dp", "ctx", None),
            P("dp", "ctx", None),
            P("dp", "ctx", None),
            P("ctx", "dp"),
            P(),
            P(),
        ),
        check_vma=False,
    )
```

time: 1010 us -> 315 us (0.31)
  waiting for transfers between devices: 725 us -> 97.7 us
  starting transfers between devices: 11.3 us -> 92 us
  local copies, waits for them, and re-layouts: 107 us -> 27.1 us
  blocking collectives: 73.6 us -> 0 us
    reduce_scatter x3 -> x0, waiting for transfers between devices: 378 us -> none  [the longest x1 141 us: shards(): lax.psum_scatter(value_terms, 'ctx', scatter_dimension=0, tiled=True)]
    all_gather x2 -> x0, waiting for transfers between devices: 194 us -> none  [the longest x1 97.3 us: shards(): lax.all_gather(attn_values, 'ctx', axis=1, tiled=True)]
    psum x1 -> x0, waiting for transfers between devices: 125 us -> none  [shards(): grad_taps, grad_gain = lax.psum((local_taps, local_gain), ('dp', 'ctx'))]
    ppermute x4 -> x45, waiting for transfers between devices: 4.52 us -> 88 us  [the longest x41 84.6 us: swap(): return lax.ppermute(block, axis, [(i, i ^ mask) for i in range(count)])]
    ppermute x4 -> x45, starting transfers between devices: 10.8 us -> 92 us  [the longest x41 84 us: swap(): return lax.ppermute(block, axis, [(i, i ^ mask) for i in range(count)])]
    psum x1 -> x0, blocking collectives: 73.6 us -> none  [shards(): grad_taps, grad_gain = lax.psum((local_taps, local_gain), ('dp', 'ctx'))]
    dynamic_slice x42 -> x3, local copies, waits for them, and re-layouts: 35.7 us -> 2.49 us  [the longest x2 1.31 us: halve(): kept = lax.dynamic_index_in_dim(block, mine, dim, keepdims=False)]
    another operation x34 -> x32, local copies, waits for them, and re-layouts: 33.3 us -> 0.53 us  [shards(): summed = sum_everywhere(jnp.stack(local_taps + [local_gain]), ctx, dp)]
  transfers between devices with their start and end apart: 12 -> 46, of which waited for: 9 -> 29; matrix products, arithmetic and copies ran while one was open for 16% -> 25% of each run, Pallas kernels for 0% -> 0%
where the time goes in v1:
time: 315 us; the launch traced here: 310 us
  waiting for transfers between devices  97.7 us (31%)
  starting transfers between devices  92 us (29%)
  matrix products  46.3 us (15%)
  other arithmetic  29.8 us (9%)
  local copies, waits for them, and re-layouts  27.1 us (9%)
  between operations  17.1 us (5%)
    ppermute x41, waiting for transfers between devices, swap(): return lax.ppermute(block, axis, [(i, i ^ mask) for i in range(count)])  84.6 us
    ppermute x41, starting transfers between devices, swap(): return lax.ppermute(block, axis, [(i, i ^ mask) for i in range(count)])  84 us
    dot_general x3, matrix products, attention_back(): lax.dot_general(prob.astype(jnp.bfloat16), d, contract, preferred_element...  13.6 us
    unnamed x190, local copies, waits for them, and re-layouts  12.2 us
    dot_general x3, matrix products, attention_back(): lax.dot_general(d, v, (((1,), (1,)), ((), ())), preferred_element_type=jn...  9.91 us
    all_gather x1, waiting for transfers between devices, shards(): weight_all = lax.all_gather(out_weight, 'dp', axis=0, tiled=True)  9.77 us
  transfers between devices with their start and end apart: 46, of which 29 were waited for; matrix products, arithmetic and copies ran while one was open for 25% of the time, Pallas kernels for 0%

profile of v1, /device:TPU:8, one launch (start us, length us, event | category | flops | bytes accessed | tf_op | source)
XLA Modules:
  0.0 310.0 jit_solution(13745278003245443001)
XLA Ops:
  10.8 6.4 %collective-permute-start = (bf16[128,576]{0,1:T(8,128)(2,1)S(1)}, bf16[128,576]{0,1:T(8,128)(2,1)S(1)}, u32[]{:S(2)}, u32[]{:S(2)}) collective-permute-start(bf16[128,576]{0,1:T(8,128)(2,1)S(1)} %get-tuple-element.141), channel_id=1, source_target_pairs={{0,24},{1,25},{2,26},{3,27},{4,28},{5,29},{6,30},{7,31},{8,16},{9,... | collective-permute-start | bytes 442376 | tf_op jit(solution)/shard_map/ppermute | solution.py:23
  19.6 10.2 %collective-permute-done = bf16[128,576]{0,1:T(8,128)(2,1)S(1)} collective-permute-done((bf16[128,576]{0,1:T(8,128)(2,1)S(1)}, bf16[128,576]{0,1:T(8,128)(2,1)S(1)}, u32[]{:S(2)}, u32[]{:S(2)}) %collective-permute-start) | collective-permute-done | bytes 147488 | tf_op jit(solution)/shard_map/ppermute | solution.py:23
  30.2 3.0 collective-permute-done.2
  34.2 3.0 collective-permute-start.3
  37.3 8.0 %collective-permute-done.4 = bf16[512,384]{0,1:T(8,128)(2,1)S(1)} collective-permute-done((bf16[512,384]{0,1:T(8,128)(2,1)S(1)}, bf16[512,384]{0,1:T(8,128)(2,1)S(1)}, u32[]{:S(2)}, u32[]{:S(2)}) %collective-permute-start.4) | collective-permute-done | bytes 393248 | tf_op jit(solution)/shard_map/ppermute | solution.py:23
  45.3 3.1 %collective-permute-start.5 = (bf16[256,384]{0,1:T(8,128)(2,1)S(1)}, bf16[256,384]{0,1:T(8,128)(2,1)S(1)}, u32[]{:S(2)}, u32[]{:S(2)}) collective-permute-start(bf16[256,384]{0,1:T(8,128)(2,1)S(1)} %slice.1056), channel_id=1, source_target_pairs={{0,2},{1,3},{2,0},{3,1},{4,6},{5,7},{6,4},{7,5},{8,10},{9,11},{10,... | collective-permute-start | bytes 589832 | tf_op jit(solution)/shard_map/ppermute | solution.py:23
  50.5 2.3 collective-permute-done.5
  55.6 3.0 collective-permute-start.13
  62.1 2.1 slice_reduce_fusion.30
  64.2 2.6 slice_reduce_fusion.31
  84.6 4.7 %collective-permute-start.10 = (bf16[128,192]{0,1:T(8,128)(2,1)S(1)}, bf16[128,192]{0,1:T(8,128)(2,1)S(1)}, u32[]{:S(2)}, u32[]{:S(2)}) collective-permute-start(bf16[128,192]{0,1:T(8,128)(2,1)S(1)} %get-tuple-element.167), channel_id=1, source_target_pairs={{0,8},{1,9},{2,10},{3,11},{4,12},{5,13},{6,14},{7,15},{8,0},{9,1},... | collective-permute-start | bytes 147464 | tf_op jit(solution)/shard_map/ppermute | solution.py:23
  89.3 5.4 %collective-permute-start.8 = (bf16[128,192]{0,1:T(8,128)(2,1)S(1)}, bf16[128,192]{0,1:T(8,128)(2,1)S(1)}, u32[]{:S(2)}, u32[]{:S(2)}) collective-permute-start(bf16[128,192]{0,1:T(8,128)(2,1)S(1)} %get-tuple-element.168), channel_id=1, source_target_pairs={{0,24},{1,25},{2,26},{3,27},{4,28},{5,29},{6,30},{7,31},{8,16},{9,... | collective-permute-start | bytes 147464 | tf_op jit(solution)/shard_map/ppermute | solution.py:23
  94.8 2.7 collective-permute-done.8
  97.5 5.5 %collective-permute-done.9 = bf16[128,192]{0,1:T(8,128)(2,1)S(1)} collective-permute-done((bf16[128,192]{0,1:T(8,128)(2,1)S(1)}, bf16[128,192]{0,1:T(8,128)(2,1)S(1)}, u32[]{:S(2)}, u32[]{:S(2)}) %collective-permute-start.9) | collective-permute-done | bytes 49184 | tf_op jit(solution)/shard_map/ppermute | solution.py:23
  103.0 9.8 %all-gather.2.cloned.1.call-done = bf16[768,1536]{1,0:T(8,128)(2,1)} async-done(((bf16[96,1536]{1,0:T(8,128)(2,1)}), bf16[768,1536]{1,0:T(8,128)(2,1)}) %all-gather.2.cloned.1.call-update) | async-done | bytes 2359312 | tf_op jit(solution)/shard_map/all_gather | solution.py:171
  113.1 2.3 fusion.154
  120.1 3.3 %collective-permute-done.12 = bf16[32,1536]{1,0:T(8,128)(2,1)S(1)} collective-permute-done((bf16[32,1536]{1,0:T(8,128)(2,1)S(1)}, bf16[32,1536]{1,0:T(8,128)(2,1)S(1)}, u32[]{:S(2)}, u32[]{:S(2)}) %collective-permute-start.12) | collective-permute-done | bytes 98336 | tf_op jit(solution)/shard_map/ppermute | solution.py:42
  123.8 5.2 %multiply_convert_fusion.3 = (bf16[160,1536]{1,0:T(8,128)(2,1)S(1)}, f32[160,1536]{1,0:T(8,128)S(1)}) fusion(bf16[16,1536]{1,0:T(8,128)(2,1)} %collective-permute-done.14, bf16[128,1536]{1,0:T(8,128)(2,1)S(1)} %bitcast.165, bf16[16,1536]{1,0:T(8,128)(2,1)} %collective-permute-done.13, bf16[192,1536]{1,0:T(8,128)(2,1)S(1)} %pad_maximum_fusion, ...), kind=kLoop, calls=%fused_computation.121 | loop fusion | flops 26296320 | bytes 17393664 | tf_op jit(solution)/shard_map/convert_element_type | solution.py:229
  129.0 5.1 %multiply_reduce_fusion = (f32[1536]{0:T(1024)S(1)}, f32[128]{0:T(128)S(1)}, f32[128,1536]{1,0:T(8,128)S(1)}) fusion(f32[128,1536]{1,0:T(8,128)S(1)} %get-tuple-element.245, f32[128]{0:T(128)S(1)} %fusion.143, f32[128]{0:T(128)S(1)} %broadcast_multiply_fusion, f32[1536]{0:T(1024)S(1)} %copy-done.32, f32[128]{0:T(128)S(1)} %copy-done.71, ...), kind=kLoop, calls=%fused_computation.174 | loop fusion | flops 19659136 | bytes 13967360 | tf_op jit(solution)/shard_map/transpose(jvp())/reduce_sum | solution.py:50
  138.4 4.8 %collective-permute-start.34 = (f32[16,1536]{1,0:T(8,128)S(1)}, f32[16,1536]{1,0:T(8,128)}, u32[]{:S(2)}, u32[]{:S(2)}) collective-permute-start(f32[16,1536]{1,0:T(8,128)S(1)} %dynamic-slice_bitcast_fusion.3), channel_id=1, source_target_pairs={{0,1},{1,0},{2,3},{3,2},{4,5},{5,4},{6,7},{7,6},{8,9},{9,8},{10,11... | collective-permute-start | bytes 294920 | tf_op jit(solution)/shard_map/ppermute | solution.py:23
  147.6 4.2 %collective-permute-start.15 = (bf16[128,192]{0,1:T(8,128)(2,1)S(1)}, bf16[128,192]{0,1:T(8,128)(2,1)S(1)}, u32[]{:S(2)}, u32[]{:S(2)}) collective-permute-start(bf16[128,192]{0,1:T(8,128)(2,1)S(1)} %get-tuple-element.163), channel_id=1, source_target_pairs={{0,24},{1,25},{2,26},{3,27},{4,28},{5,29},{6,30},{7,31},{8,16},{9,... | collective-permute-start | bytes 147464 | tf_op jit(solution)/shard_map/ppermute | solution.py:23
  151.8 2.0 collective-permute-start.16
  156.8 3.4 %collective-permute-done.16 = bf16[128,192]{0,1:T(8,128)(2,1)S(1)} collective-permute-done((bf16[128,192]{0,1:T(8,128)(2,1)S(1)}, bf16[128,192]{0,1:T(8,128)(2,1)S(1)}, u32[]{:S(2)}, u32[]{:S(2)}) %collective-permute-start.16) | collective-permute-done | bytes 49184 | tf_op jit(solution)/shard_map/ppermute | solution.py:23
  160.8 2.4 multiply_convert_fusion.2
  163.3 3.8 %multiply_convert_fusion.1 = bf16[512,4096]{1,0:T(8,128)(2,1)} fusion(f32[512,4096]{1,0:T(8,128)S(1)} %bitcast.154, f32[512]{0:T(512)S(1)} %bitcast.188, f32[512]{0:T(512)S(1)} %log_add_fusion.1, bf16[4096,384]{0,1:T(8,128)(2,1)S(1)} %copy-done.9, bf16[512,192]{0,1:T(8,128)(2,1)S(1)} %pad_maximum_fusion.13), kind=kOutput, calls=%fused_computation.2 | convolution fusion | flops 276824064 | bytes 13176832 | tf_op jit(solution)/shard_map/dot_general | solution.py:101
  168.6 3.7 %multiply_convert_fusion = bf16[512,4096]{1,0:T(8,128)(2,1)} fusion(f32[512,4096]{1,0:T(8,128)S(1)} %bitcast.150, f32[512]{0:T(512)S(1)} %bitcast.187, f32[512]{0:T(512)S(1)} %copy-done.66, bf16[4096,384]{0,1:T(8,128)(2,1)S(1)} %copy-done.9, bf16[512,192]{0,1:T(8,128)(2,1)S(1)} %pad_maximum_fusion.13), kind=kOutput, calls=%fused_computation | convolution fusion | flops 276824064 | bytes 13176832 | tf_op jit(solution)/shard_map/dot_general | solution.py:101
  173.2 2.9 collective-permute-start.35
  183.3 5.7 %fusion.7 = bf16[4096,384]{0,1:T(8,128)(2,1)} fusion(bf16[4096,384]{0,1:T(8,128)(2,1)} %fusion.6, f32[512,4096]{1,0:T(8,128)} %copy-done.2, f32[512]{0:T(512)S(1)} %copy-done.65, bf16[512,192]{0,1:T(8,128)(2,1)} %copy-done.17), kind=kOutput, calls=%fused_computation.60 | convolution fusion | flops 272891904 | bytes 8980480 | tf_op jit(solution)/shard_map/dot_general | solution.py:117
  194.2 3.1 %collective-permute-start.38 = (f32[4,1536]{1,0:T(4,128)S(1)}, f32[4,1536]{1,0:T(4,128)S(1)}, u32[]{:S(2)}, u32[]{:S(2)}) collective-permute-start(f32[4,1536]{1,0:T(4,128)S(1)} %add.649), channel_id=1, source_target_pairs={{0,16},{1,17},{2,18},{3,19},{4,20},{5,21},{6,22},{7,23},{8,24},{9,... | collective-permute-start | bytes 73736 | tf_op jit(solution)/shard_map/ppermute | solution.py:23
  197.3 5.6 %fusion.9 = bf16[4096,384]{0,1:T(8,128)(2,1)} fusion(bf16[4096,384]{0,1:T(8,128)(2,1)} %fusion.8, f32[512,4096]{1,0:T(8,128)} %copy-done.1, f32[512]{0:T(512)S(1)} %copy-done.63, bf16[512,192]{0,1:T(8,128)(2,1)S(1)} %copy-done.18), kind=kOutput, calls=%fused_computation.62 | convolution fusion | flops 272891904 | bytes 8980480 | tf_op jit(solution)/shard_map/dot_general | solution.py:117
  206.9 2.5 collective-permute-start.40
  209.4 2.3 fusion.11
  214.6 2.5 collective-permute-done.41
  221.1 3.4 %collective-permute-start.43 = (f32[8,1536]{1,0:T(8,128)S(1)}, f32[8,1536]{1,0:T(8,128)S(1)}, u32[]{:S(2)}, u32[]{:S(2)}) collective-permute-start(f32[8,1536]{1,0:T(8,128)S(1)} %pad_maximum_fusion.15), channel_id=1, source_target_pairs={{0,2},{1,3},{2,0},{3,1},{4,6},{5,7},{6,4},{7,5},{8,10},{9,11},{10,... | collective-permute-start | bytes 147464 | tf_op jit(solution)/shard_map/ppermute | solution.py:23
  228.6 3.4 %collective-permute-start.27 = (bf16[2,2,2,24,1536]{4,3,0,1,2:T(8,128)(2,1)S(1)}, bf16[2,2,2,24,1536]{4,3,0,1,2:T(8,128)(2,1)S(1)}, u32[]{:S(2)}, u32[]{:S(2)}) collective-permute-start(bf16[2,2,2,24,1536]{4,3,0,1,2:T(8,128)(2,1)S(1)} %dynamic-slice_bitcast_fusion), channel_id=1, source_target_pairs={{0,2},{1,3},{2,0},{3,1},{4,6},{5,7},{6,4},{7,5},{8,10},{9,11},{10,... | collective-permute-start | bytes 1769480 | tf_op jit(solution)/shard_map/ppermute | solution.py:23
  233.3 12.6 %collective-permute-done.27 = bf16[2,2,2,24,1536]{4,3,0,1,2:T(8,128)(2,1)S(1)} collective-permute-done((bf16[2,2,2,24,1536]{4,3,0,1,2:T(8,128)(2,1)S(1)}, bf16[2,2,2,24,1536]{4,3,0,1,2:T(8,128)(2,1)S(1)}, u32[]{:S(2)}, u32[]{:S(2)}) %collective-permute-start.27) | collective-permute-done | bytes 589856 | tf_op jit(solution)/shard_map/ppermute | solution.py:23
  249.0 3.2 %collective-permute-start.21 = (bf16[256,384]{0,1:T(8,128)(2,1)S(1)}, bf16[256,384]{0,1:T(8,128)(2,1)S(1)}, u32[]{:S(2)}, u32[]{:S(2)}) collective-permute-start(bf16[256,384]{0,1:T(8,128)(2,1)S(1)} %get-tuple-element.122), channel_id=1, source_target_pairs={{0,2},{1,3},{2,0},{3,1},{4,6},{5,7},{6,4},{7,5},{8,10},{9,11},{10,... | collective-permute-start | bytes 589832 | tf_op jit(solution)/shard_map/ppermute | solution.py:23
  252.2 3.9 %collective-permute-done.28 = bf16[2,2,24,1536]{3,2,0,1:T(8,128)(2,1)S(1)} collective-permute-done((bf16[2,2,24,1536]{3,2,0,1:T(8,128)(2,1)S(1)}, bf16[2,2,24,1536]{3,2,0,1:T(8,128)(2,1)S(1)}, u32[]{:S(2)}, u32[]{:S(2)}) %collective-permute-start.28) | collective-permute-done | bytes 294944 | tf_op jit(solution)/shard_map/ppermute | solution.py:23
  257.7 3.0 collective-permute-done.19
  260.8 3.2 %collective-permute-start.20 = (bf16[512,384]{0,1:T(8,128)(2,1)S(1)}, bf16[512,384]{0,1:T(8,128)(2,1)S(1)}, u32[]{:S(2)}, u32[]{:S(2)}) collective-permute-start(bf16[512,384]{0,1:T(8,128)(2,1)S(1)} %pad_maximum_fusion.7), channel_id=1, source_target_pairs={{0,2},{1,3},{2,0},{3,1},{4,6},{5,7},{6,4},{7,5},{8,10},{9,11},{10,... | collective-permute-start | bytes 1179656 | tf_op jit(solution)/shard_map/ppermute | solution.py:23
  264.4 3.1 %collective-permute-start.30 = (bf16[24,1536]{1,0:T(8,128)(2,1)S(1)}, bf16[24,1536]{1,0:T(8,128)(2,1)S(1)}, u32[]{:S(2)}, u32[]{:S(2)}) collective-permute-start(bf16[24,1536]{1,0:T(8,128)(2,1)S(1)} %dynamic-slice_bitcast_fusion.4), channel_id=1, source_target_pairs={{0,16},{1,17},{2,18},{3,19},{4,20},{5,21},{6,22},{7,23},{8,24},{9,... | collective-permute-start | bytes 221192 | tf_op jit(solution)/shard_map/ppermute | solution.py:23
  267.7 7.0 %collective-permute-done.30 = bf16[24,1536]{1,0:T(8,128)(2,1)S(1)} collective-permute-done((bf16[24,1536]{1,0:T(8,128)(2,1)S(1)}, bf16[24,1536]{1,0:T(8,128)(2,1)S(1)}, u32[]{:S(2)}, u32[]{:S(2)}) %collective-permute-start.30) | collective-permute-done | bytes 73760 | tf_op jit(solution)/shard_map/ppermute | solution.py:23
  277.9 2.6 collective-permute-done.31
  282.2 2.2 collective-permute-done.32
  285.5 2.8 collective-permute-start.24
  288.4 3.7 %collective-permute-start.25 = (bf16[128,576]{0,1:T(8,128)(2,1)S(1)}, bf16[128,576]{0,1:T(8,128)(2,1)S(1)}, u32[]{:S(2)}, u32[]{:S(2)}) collective-permute-start(bf16[128,576]{0,1:T(8,128)(2,1)S(1)} %get-tuple-element.134), channel_id=1, source_target_pairs={{0,8},{1,9},{2,10},{3,11},{4,12},{5,13},{6,14},{7,15},{8,0},{9,1},... | collective-permute-start | bytes 442376 | tf_op jit(solution)/shard_map/ppermute | solution.py:23
  294.2 2.4 collective-permute-done.24
  296.6 3.5 %collective-permute-done.25 = bf16[128,576]{0,1:T(8,128)(2,1)S(1)} collective-permute-done((bf16[128,576]{0,1:T(8,128)(2,1)S(1)}, bf16[128,576]{0,1:T(8,128)(2,1)S(1)}, u32[]{:S(2)}, u32[]{:S(2)}) %collective-permute-start.25) | collective-permute-done | bytes 147488 | tf_op jit(solution)/shard_map/ppermute | solution.py:23
  (398 shorter events, 96.2 us)
Async XLA Ops:
  7.2 105.7 %all-gather.2.cloned.1.call-start = ((), (), s32[]{:S(2)}) async-start(), calls=%async_computation | async-start | bytes 2654208 | tf_op jit(solution)/shard_map/all_gather | solution.py:171
  10.8 19.0 %collective-permute-start = (bf16[128,576]{0,1:T(8,128)(2,1)S(1)}, bf16[128,576]{0,1:T(8,128)(2,1)S(1)}, u32[]{:S(2)}, u32[]{:S(2)}) collective-permute-start(bf16[128,576]{0,1:T(8,128)(2,1)S(1)} %get-tuple-element.141), channel_id=1, source_target_pairs={{0,24},{1,25},{2,26},{3,27},{4,28},{5,29},{6,30},{7,31},{8,16},{9,... | collective-permute-start | bytes 442376 | tf_op jit(solution)/shard_map/ppermute | solution.py:23
  17.2 13.0 %collective-permute-start.1 = (bf16[128,576]{0,1:T(8,128)(2,1)S(1)}, bf16[128,576]{0,1:T(8,128)(2,1)S(1)}, u32[]{:S(2)}, u32[]{:S(2)}) collective-permute-start(bf16[128,576]{0,1:T(8,128)(2,1)S(1)} %get-tuple-element.140), channel_id=1, source_target_pairs={{0,16},{1,17},{2,18},{3,19},{4,20},{5,21},{6,22},{7,23},{8,24},{9,... | collective-permute-start | bytes 442376 | tf_op jit(solution)/shard_map/ppermute | solution.py:23
  18.2 15.0 %collective-permute-start.2 = (bf16[128,576]{0,1:T(8,128)(2,1)S(1)}, bf16[128,576]{0,1:T(8,128)(2,1)S(1)}, u32[]{:S(2)}, u32[]{:S(2)}) collective-permute-start(bf16[128,576]{0,1:T(8,128)(2,1)S(1)} %get-tuple-element.139), channel_id=1, source_target_pairs={{0,8},{1,9},{2,10},{3,11},{4,12},{5,13},{6,14},{7,15},{8,0},{9,1},... | collective-permute-start | bytes 442376 | tf_op jit(solution)/shard_map/ppermute | solution.py:23
  34.2 11.0 %collective-permute-start.4 = (bf16[512,384]{0,1:T(8,128)(2,1)S(1)}, bf16[512,384]{0,1:T(8,128)(2,1)S(1)}, u32[]{:S(2)}, u32[]{:S(2)}) collective-permute-start(bf16[512,384]{0,1:T(8,128)(2,1)S(1)} %get-tuple-element.113), channel_id=1, source_target_pairs={{0,4},{1,5},{2,6},{3,7},{4,0},{5,1},{6,2},{7,3},{8,12},{9,13},{10,... | collective-permute-start | bytes 1179656 | tf_op jit(solution)/shard_map/ppermute | solution.py:23
  34.2 14.2 %collective-permute-start.3 = (bf16[512,384]{0,1:T(8,128)(2,1)S(1)}, bf16[512,384]{0,1:T(8,128)(2,1)S(1)}, u32[]{:S(2)}, u32[]{:S(2)}) collective-permute-start(bf16[512,384]{0,1:T(8,128)(2,1)S(1)} %get-tuple-element.113), channel_id=1, source_target_pairs={{0,2},{1,3},{2,0},{3,1},{4,6},{5,7},{6,4},{7,5},{8,10},{9,11},{10,... | collective-permute-start | bytes 1179656 | tf_op jit(solution)/shard_map/ppermute | solution.py:23
  45.3 7.6 %collective-permute-start.5 = (bf16[256,384]{0,1:T(8,128)(2,1)S(1)}, bf16[256,384]{0,1:T(8,128)(2,1)S(1)}, u32[]{:S(2)}, u32[]{:S(2)}) collective-permute-start(bf16[256,384]{0,1:T(8,128)(2,1)S(1)} %slice.1056), channel_id=1, source_target_pairs={{0,2},{1,3},{2,0},{3,1},{4,6},{5,7},{6,4},{7,5},{8,10},{9,11},{10,... | collective-permute-start | bytes 589832 | tf_op jit(solution)/shard_map/ppermute | solution.py:23
  48.4 5.8 %collective-permute-start.6 = (bf16[256,384]{0,1:T(8,128)(2,1)S(1)}, bf16[256,384]{0,1:T(8,128)(2,1)S(1)}, u32[]{:S(2)}, u32[]{:S(2)}) collective-permute-start(bf16[256,384]{0,1:T(8,128)(2,1)S(1)} %slice.1057), channel_id=1, source_target_pairs={{0,4},{1,5},{2,6},{3,7},{4,0},{5,1},{6,2},{7,3},{8,12},{9,13},{10,... | collective-permute-start | bytes 589832 | tf_op jit(solution)/shard_map/ppermute | solution.py:23
  54.9 13.5 %collective-permute-start.7 = (bf16[2048,384]{0,1:T(8,128)(2,1)}, bf16[2048,384]{0,1:T(8,128)(2,1)}, u32[]{:S(2)}, u32[]{:S(2)}) collective-permute-start(bf16[2048,384]{0,1:T(8,128)(2,1)} %get-tuple-element.169), channel_id=1, source_target_pairs={{0,1},{1,0},{2,3},{3,2},{4,5},{5,4},{6,7},{7,6},{8,9},{9,8},{10,11... | collective-permute-start | bytes 4718600 | tf_op jit(solution)/shard_map/ppermute | solution.py:23
  55.6 67.9 %collective-permute-start.13 = (bf16[16,1536]{1,0:T(8,128)(2,1)}, bf16[16,1536]{1,0:T(8,128)(2,1)}, u32[]{:S(2)}, u32[]{:S(2)}) collective-permute-start(bf16[16,1536]{1,0:T(8,128)(2,1)} %get-tuple-element.144), channel_id=1, source_target_pairs={{0,1},{1,2},{2,3},{3,4},{4,5},{5,6},{6,7},{7,8},{8,9},{9,10},{10,1... | collective-permute-start | bytes 147464 | tf_op jit(solution)/shard_map/ppermute | solution.py:41
  58.6 64.9 %collective-permute-start.14 = (bf16[16,1536]{1,0:T(8,128)(2,1)}, bf16[16,1536]{1,0:T(8,128)(2,1)}, u32[]{:S(2)}, u32[]{:S(2)}) collective-permute-start(bf16[16,1536]{1,0:T(8,128)(2,1)} %get-tuple-element.145), channel_id=1, source_target_pairs={{1,0},{2,1},{3,2},{4,3},{5,4},{6,5},{7,6},{8,7},{9,8},{10,9},{11,1... | collective-permute-start | bytes 147464 | tf_op jit(solution)/shard_map/ppermute | solution.py:42
  84.6 10.2 %collective-permute-start.10 = (bf16[128,192]{0,1:T(8,128)(2,1)S(1)}, bf16[128,192]{0,1:T(8,128)(2,1)S(1)}, u32[]{:S(2)}, u32[]{:S(2)}) collective-permute-start(bf16[128,192]{0,1:T(8,128)(2,1)S(1)} %get-tuple-element.167), channel_id=1, source_target_pairs={{0,8},{1,9},{2,10},{3,11},{4,12},{5,13},{6,14},{7,15},{8,0},{9,1},... | collective-permute-start | bytes 147464 | tf_op jit(solution)/shard_map/ppermute | solution.py:23
  89.3 8.1 %collective-permute-start.8 = (bf16[128,192]{0,1:T(8,128)(2,1)S(1)}, bf16[128,192]{0,1:T(8,128)(2,1)S(1)}, u32[]{:S(2)}, u32[]{:S(2)}) collective-permute-start(bf16[128,192]{0,1:T(8,128)(2,1)S(1)} %get-tuple-element.168), channel_id=1, source_target_pairs={{0,24},{1,25},{2,26},{3,27},{4,28},{5,29},{6,30},{7,31},{8,16},{9,... | collective-permute-start | bytes 147464 | tf_op jit(solution)/shard_map/ppermute | solution.py:23
  94.7 8.2 %collective-permute-start.9 = (bf16[128,192]{0,1:T(8,128)(2,1)S(1)}, bf16[128,192]{0,1:T(8,128)(2,1)S(1)}, u32[]{:S(2)}, u32[]{:S(2)}) collective-permute-start(bf16[128,192]{0,1:T(8,128)(2,1)S(1)} %get-tuple-element.109), channel_id=1, source_target_pairs={{0,16},{1,17},{2,18},{3,19},{4,20},{5,21},{6,22},{7,23},{8,24},{9,... | collective-permute-start | bytes 147464 | tf_op jit(solution)/shard_map/ppermute | solution.py:23
  94.8 66.0 %copy-start.64 = (f32[512]{0:T(512)}, f32[512]{0:T(512)S(1)}, u32[]{:S(2)}) copy-start(f32[512]{0:T(512)S(1)} %log_add_fusion.2) | copy-start | bytes 6148
  94.8 68.4 %copy-start.62 = (f32[512]{0:T(512)}, f32[512]{0:T(512)S(1)}, u32[]{:S(2)}) copy-start(f32[512]{0:T(512)S(1)} %log_add_fusion.1) | copy-start | bytes 6148
  116.0 4.1 %collective-permute-start.11 = (bf16[32,1536]{1,0:T(8,128)(2,1)S(1)}, bf16[32,1536]{1,0:T(8,128)(2,1)S(1)}, u32[]{:S(2)}, u32[]{:S(2)}) collective-permute-start(bf16[32,1536]{1,0:T(8,128)(2,1)S(1)} %get-tuple-element.142), channel_id=1, source_target_pairs={{0,1},{1,2},{2,3},{3,4},{4,5},{5,6},{6,7},{7,8},{8,9},{9,10},{10,1... | collective-permute-start | bytes 294920 | tf_op jit(solution)/shard_map/ppermute | solution.py:41
  117.8 5.7 %collective-permute-start.12 = (bf16[32,1536]{1,0:T(8,128)(2,1)S(1)}, bf16[32,1536]{1,0:T(8,128)(2,1)S(1)}, u32[]{:S(2)}, u32[]{:S(2)}) collective-permute-start(bf16[32,1536]{1,0:T(8,128)(2,1)S(1)} %get-tuple-element.143), channel_id=1, source_target_pairs={{1,0},{2,1},{3,2},{4,3},{5,4},{6,5},{7,6},{8,7},{9,8},{10,9},{11,1... | collective-permute-start | bytes 294920 | tf_op jit(solution)/shard_map/ppermute | solution.py:42
  138.4 33.9 %collective-permute-start.34 = (f32[16,1536]{1,0:T(8,128)S(1)}, f32[16,1536]{1,0:T(8,128)}, u32[]{:S(2)}, u32[]{:S(2)}) collective-permute-start(f32[16,1536]{1,0:T(8,128)S(1)} %dynamic-slice_bitcast_fusion.3), channel_id=1, source_target_pairs={{0,1},{1,0},{2,3},{3,2},{4,5},{5,4},{6,7},{7,6},{8,9},{9,8},{10,11... | collective-permute-start | bytes 294920 | tf_op jit(solution)/shard_map/ppermute | solution.py:23
  147.6 9.3 %collective-permute-start.15 = (bf16[128,192]{0,1:T(8,128)(2,1)S(1)}, bf16[128,192]{0,1:T(8,128)(2,1)S(1)}, u32[]{:S(2)}, u32[]{:S(2)}) collective-permute-start(bf16[128,192]{0,1:T(8,128)(2,1)S(1)} %get-tuple-element.163), channel_id=1, source_target_pairs={{0,24},{1,25},{2,26},{3,27},{4,28},{5,29},{6,30},{7,31},{8,16},{9,... | collective-permute-start | bytes 147464 | tf_op jit(solution)/shard_map/ppermute | solution.py:23
  151.8 8.5 %collective-permute-start.16 = (bf16[128,192]{0,1:T(8,128)(2,1)S(1)}, bf16[128,192]{0,1:T(8,128)(2,1)S(1)}, u32[]{:S(2)}, u32[]{:S(2)}) collective-permute-start(bf16[128,192]{0,1:T(8,128)(2,1)S(1)} %get-tuple-element.164), channel_id=1, source_target_pairs={{0,16},{1,17},{2,18},{3,19},{4,20},{5,21},{6,22},{7,23},{8,24},{9,... | collective-permute-start | bytes 147464 | tf_op jit(solution)/shard_map/ppermute | solution.py:23
  153.8 6.7 %collective-permute-start.17 = (bf16[128,192]{0,1:T(8,128)(2,1)S(1)}, bf16[128,192]{0,1:T(8,128)(2,1)S(1)}, u32[]{:S(2)}, u32[]{:S(2)}) collective-permute-start(bf16[128,192]{0,1:T(8,128)(2,1)S(1)} %get-tuple-element.162), channel_id=1, source_target_pairs={{0,8},{1,9},{2,10},{3,11},{4,12},{5,13},{6,14},{7,15},{8,0},{9,1},... | collective-permute-start | bytes 147464 | tf_op jit(solution)/shard_map/ppermute | solution.py:23
  156.8 70.1 %collective-permute-start.26 = (bf16[2,2,2,2,24,1536]{5,4,0,1,2,3:T(8,128)(2,1)}, bf16[2,2,2,2,24,1536]{5,4,0,1,2,3:T(8,128)(2,1)}, u32[]{:S(2)}, u32[]{:S(2)}) collective-permute-start(bf16[2,2,2,2,24,1536]{5,4,0,1,2,3:T(8,128)(2,1)} %bitcast.143), channel_id=1, source_target_pairs={{0,1},{1,0},{2,3},{3,2},{4,5},{5,4},{6,7},{7,6},{8,9},{9,8},{10,11... | collective-permute-start | bytes 3538952 | tf_op jit(solution)/shard_map/ppermute | solution.py:23
  173.2 5.7 %collective-permute-start.35 = (f32[8,1536]{1,0:T(8,128)S(1)}, f32[8,1536]{1,0:T(8,128)S(1)}, u32[]{:S(2)}, u32[]{:S(2)}) collective-permute-start(f32[8,1536]{1,0:T(8,128)S(1)} %dynamic-slice_bitcast_fusion.5), channel_id=1, source_target_pairs={{0,2},{1,3},{2,0},{3,1},{4,6},{5,7},{6,4},{7,5},{8,10},{9,11},{10,... | collective-permute-start | bytes 147464 | tf_op jit(solution)/shard_map/ppermute | solution.py:23
  181.7 7.3 %collective-permute-start.36 = (f32[4,1536]{1,0:T(4,128)S(1)}, f32[4,1536]{1,0:T(4,128)S(1)}, u32[]{:S(2)}, u32[]{:S(2)}) collective-permute-start(f32[4,1536]{1,0:T(4,128)S(1)} %dynamic-slice_bitcast_fusion.6), channel_id=1, source_target_pairs={{0,4},{1,5},{2,6},{3,7},{4,0},{5,1},{6,2},{7,3},{8,12},{9,13},{10,... | collective-permute-start | bytes 73736 | tf_op jit(solution)/shard_map/ppermute | solution.py:23
  189.1 5.1 %collective-permute-start.37 = (f32[4,1536]{1,0:T(4,128)S(1)}, f32[4,1536]{1,0:T(4,128)S(1)}, u32[]{:S(2)}, u32[]{:S(2)}) collective-permute-start(f32[4,1536]{1,0:T(4,128)S(1)} %bitcast_add_fusion.4), channel_id=1, source_target_pairs={{0,8},{1,9},{2,10},{3,11},{4,12},{5,13},{6,14},{7,15},{8,0},{9,1},... | collective-permute-start | bytes 73736 | tf_op jit(solution)/shard_map/ppermute | solution.py:23
  194.2 8.8 %collective-permute-start.38 = (f32[4,1536]{1,0:T(4,128)S(1)}, f32[4,1536]{1,0:T(4,128)S(1)}, u32[]{:S(2)}, u32[]{:S(2)}) collective-permute-start(f32[4,1536]{1,0:T(4,128)S(1)} %add.649), channel_id=1, source_target_pairs={{0,16},{1,17},{2,18},{3,19},{4,20},{5,21},{6,22},{7,23},{8,24},{9,... | collective-permute-start | bytes 73736 | tf_op jit(solution)/shard_map/ppermute | solution.py:23
  203.0 3.9 %collective-permute-start.39 = (f32[4,1536]{1,0:T(4,128)S(1)}, f32[4,1536]{1,0:T(4,128)S(1)}, u32[]{:S(2)}, u32[]{:S(2)}) collective-permute-start(f32[4,1536]{1,0:T(4,128)S(1)} %add.650), channel_id=1, source_target_pairs={{0,32},{32,0},{64,96},{96,64},{128,160},{160,128},{192,224},{224,1... | collective-permute-start | bytes 73736 | tf_op jit(solution)/shard_map/ppermute | solution.py:23
  206.9 4.8 %collective-permute-start.40 = (f32[4,1536]{1,0:T(4,128)S(1)}, f32[4,1536]{1,0:T(4,128)S(1)}, u32[]{:S(2)}, u32[]{:S(2)}) collective-permute-start(f32[4,1536]{1,0:T(4,128)S(1)} %add.651), channel_id=1, source_target_pairs={{0,64},{32,96},{64,0},{96,32},{128,192},{160,224},{192,128},{224,1... | collective-permute-start | bytes 73736 | tf_op jit(solution)/shard_map/ppermute | solution.py:23
  211.7 5.4 %collective-permute-start.41 = (f32[4,1536]{1,0:T(4,128)S(1)}, f32[4,1536]{1,0:T(4,128)S(1)}, u32[]{:S(2)}, u32[]{:S(2)}) collective-permute-start(f32[4,1536]{1,0:T(4,128)S(1)} %add.652), channel_id=1, source_target_pairs={{0,128},{32,160},{64,192},{96,224},{128,0},{160,32},{192,64},{224,... | collective-permute-start | bytes 73736 | tf_op jit(solution)/shard_map/ppermute | solution.py:23
  217.1 3.9 %collective-permute-start.42 = (f32[4,1536]{1,0:T(4,128)S(1)}, f32[4,1536]{1,0:T(4,128)S(1)}, u32[]{:S(2)}, u32[]{:S(2)}) collective-permute-start(f32[4,1536]{1,0:T(4,128)S(1)} %add.653), channel_id=1, source_target_pairs={{0,4},{1,5},{2,6},{3,7},{4,0},{5,1},{6,2},{7,3},{8,12},{9,13},{10,... | collective-permute-start | bytes 73736 | tf_op jit(solution)/shard_map/ppermute | solution.py:23
  221.1 5.7 %collective-permute-start.43 = (f32[8,1536]{1,0:T(8,128)S(1)}, f32[8,1536]{1,0:T(8,128)S(1)}, u32[]{:S(2)}, u32[]{:S(2)}) collective-permute-start(f32[8,1536]{1,0:T(8,128)S(1)} %pad_maximum_fusion.15), channel_id=1, source_target_pairs={{0,2},{1,3},{2,0},{3,1},{4,6},{5,7},{6,4},{7,5},{8,10},{9,11},{10,... | collective-permute-start | bytes 147464 | tf_op jit(solution)/shard_map/ppermute | solution.py:23
  226.0 21.4 %collective-permute-start.18 = (bf16[2048,384]{0,1:T(8,128)(2,1)S(1)}, bf16[2048,384]{0,1:T(8,128)(2,1)S(1)}, u32[]{:S(2)}, u32[]{:S(2)}) collective-permute-start(bf16[2048,384]{0,1:T(8,128)(2,1)S(1)} %slice.1147), channel_id=1, source_target_pairs={{0,1},{1,0},{2,3},{3,2},{4,5},{5,4},{6,7},{7,6},{8,9},{9,8},{10,11... | collective-permute-start | bytes 4718600 | tf_op jit(solution)/shard_map/ppermute | solution.py:23
  226.8 5.1 %collective-permute-start.44 = (f32[16,1536]{1,0:T(8,128)S(1)}, f32[16,1536]{1,0:T(8,128)S(1)}, u32[]{:S(2)}, u32[]{:S(2)}) collective-permute-start(f32[16,1536]{1,0:T(8,128)S(1)} %pad_maximum_fusion.14), channel_id=1, source_target_pairs={{0,1},{1,0},{2,3},{3,2},{4,5},{5,4},{6,7},{7,6},{8,9},{9,8},{10,11... | collective-permute-start | bytes 294920 | tf_op jit(solution)/shard_map/ppermute | solution.py:23
  228.6 17.3 %collective-permute-start.27 = (bf16[2,2,2,24,1536]{4,3,0,1,2:T(8,128)(2,1)S(1)}, bf16[2,2,2,24,1536]{4,3,0,1,2:T(8,128)(2,1)S(1)}, u32[]{:S(2)}, u32[]{:S(2)}) collective-permute-start(bf16[2,2,2,24,1536]{4,3,0,1,2:T(8,128)(2,1)S(1)} %dynamic-slice_bitcast_fusion), channel_id=1, source_target_pairs={{0,2},{1,3},{2,0},{3,1},{4,6},{5,7},{6,4},{7,5},{8,10},{9,11},{10,... | collective-permute-start | bytes 1769480 | tf_op jit(solution)/shard_map/ppermute | solution.py:23
  246.1 10.0 %collective-permute-start.28 = (bf16[2,2,24,1536]{3,2,0,1:T(8,128)(2,1)S(1)}, bf16[2,2,24,1536]{3,2,0,1:T(8,128)(2,1)S(1)}, u32[]{:S(2)}, u32[]{:S(2)}) collective-permute-start(bf16[2,2,24,1536]{3,2,0,1:T(8,128)(2,1)S(1)} %dynamic-slice_bitcast_fusion.1), channel_id=1, source_target_pairs={{0,4},{1,5},{2,6},{3,7},{4,0},{5,1},{6,2},{7,3},{8,12},{9,13},{10,... | collective-permute-start | bytes 884744 | tf_op jit(solution)/shard_map/ppermute | solution.py:23
  248.1 12.5 %collective-permute-start.19 = (bf16[256,384]{0,1:T(8,128)(2,1)S(1)}, bf16[256,384]{0,1:T(8,128)(2,1)S(1)}, u32[]{:S(2)}, u32[]{:S(2)}) collective-permute-start(bf16[256,384]{0,1:T(8,128)(2,1)S(1)} %get-tuple-element.123), channel_id=1, source_target_pairs={{0,4},{1,5},{2,6},{3,7},{4,0},{5,1},{6,2},{7,3},{8,12},{9,13},{10,... | collective-permute-start | bytes 589832 | tf_op jit(solution)/shard_map/ppermute | solution.py:23
  249.0 11.6 %collective-permute-start.21 = (bf16[256,384]{0,1:T(8,128)(2,1)S(1)}, bf16[256,384]{0,1:T(8,128)(2,1)S(1)}, u32[]{:S(2)}, u32[]{:S(2)}) collective-permute-start(bf16[256,384]{0,1:T(8,128)(2,1)S(1)} %get-tuple-element.122), channel_id=1, source_target_pairs={{0,2},{1,3},{2,0},{3,1},{4,6},{5,7},{6,4},{7,5},{8,10},{9,11},{10,... | collective-permute-start | bytes 589832 | tf_op jit(solution)/shard_map/ppermute | solution.py:23
  256.2 8.2 %collective-permute-start.29 = (bf16[2,24,1536]{2,1,0:T(8,128)(2,1)S(1)}, bf16[2,24,1536]{2,1,0:T(8,128)(2,1)S(1)}, u32[]{:S(2)}, u32[]{:S(2)}) collective-permute-start(bf16[2,24,1536]{2,1,0:T(8,128)(2,1)S(1)} %dynamic-slice_bitcast_fusion.2), channel_id=1, source_target_pairs={{0,8},{1,9},{2,10},{3,11},{4,12},{5,13},{6,14},{7,15},{8,0},{9,1},... | collective-permute-start | bytes 442376 | tf_op jit(solution)/shard_map/ppermute | solution.py:23
  260.8 15.7 %collective-permute-start.20 = (bf16[512,384]{0,1:T(8,128)(2,1)S(1)}, bf16[512,384]{0,1:T(8,128)(2,1)S(1)}, u32[]{:S(2)}, u32[]{:S(2)}) collective-permute-start(bf16[512,384]{0,1:T(8,128)(2,1)S(1)} %pad_maximum_fusion.7), channel_id=1, source_target_pairs={{0,2},{1,3},{2,0},{3,1},{4,6},{5,7},{6,4},{7,5},{8,10},{9,11},{10,... | collective-permute-start | bytes 1179656 | tf_op jit(solution)/shard_map/ppermute | solution.py:23
  264.4 10.2 %collective-permute-start.30 = (bf16[24,1536]{1,0:T(8,128)(2,1)S(1)}, bf16[24,1536]{1,0:T(8,128)(2,1)S(1)}, u32[]{:S(2)}, u32[]{:S(2)}) collective-permute-start(bf16[24,1536]{1,0:T(8,128)(2,1)S(1)} %dynamic-slice_bitcast_fusion.4), channel_id=1, source_target_pairs={{0,16},{1,17},{2,18},{3,19},{4,20},{5,21},{6,22},{7,23},{8,24},{9,... | collective-permute-start | bytes 221192 | tf_op jit(solution)/shard_map/ppermute | solution.py:23
  267.6 10.1 %collective-permute-start.22 = (bf16[512,384]{0,1:T(8,128)(2,1)S(1)}, bf16[512,384]{0,1:T(8,128)(2,1)S(1)}, u32[]{:S(2)}, u32[]{:S(2)}) collective-permute-start(bf16[512,384]{0,1:T(8,128)(2,1)S(1)} %pad_maximum_fusion.8), channel_id=1, source_target_pairs={{0,4},{1,5},{2,6},{3,7},{4,0},{5,1},{6,2},{7,3},{8,12},{9,13},{10,... | collective-permute-start | bytes 1179656 | tf_op jit(solution)/shard_map/ppermute | solution.py:23
  274.9 5.5 %collective-permute-start.31 = (bf16[24,768]{1,0:T(8,128)(2,1)S(1)}, bf16[24,768]{1,0:T(8,128)(2,1)S(1)}, u32[]{:S(2)}, u32[]{:S(2)}) collective-permute-start(bf16[24,768]{1,0:T(8,128)(2,1)S(1)} %bitcast.184), channel_id=1, source_target_pairs={{0,128},{32,160},{64,192},{96,224},{128,0},{160,32},{192,64},{224,... | collective-permute-start | bytes 110600 | tf_op jit(solution)/shard_map/ppermute | solution.py:23
  280.6 3.8 %collective-permute-start.32 = (bf16[24,384]{1,0:T(8,128)(2,1)S(1)}, bf16[24,384]{1,0:T(8,128)(2,1)S(1)}, u32[]{:S(2)}, u32[]{:S(2)}) collective-permute-start(bf16[24,384]{1,0:T(8,128)(2,1)S(1)} %bitcast.185), channel_id=1, source_target_pairs={{0,64},{32,96},{64,0},{96,32},{128,192},{160,224},{192,128},{224,1... | collective-permute-start | bytes 55304 | tf_op jit(solution)/shard_map/ppermute | solution.py:23
  284.6 7.4 %collective-permute-start.33 = (bf16[24,192]{1,0:T(8,128)(2,1)S(1)}, bf16[24,192]{1,0:T(8,128)(2,1)S(1)}, u32[]{:S(2)}, u32[]{:S(2)}) collective-permute-start(bf16[24,192]{1,0:T(8,128)(2,1)S(1)} %bitcast.186), channel_id=1, source_target_pairs={{0,32},{32,0},{64,96},{96,64},{128,160},{160,128},{192,224},{224,1... | collective-permute-start | bytes 27656 | tf_op jit(solution)/shard_map/ppermute | solution.py:23
  285.4 8.8 %collective-permute-start.23 = (bf16[128,576]{0,1:T(8,128)(2,1)S(1)}, bf16[128,576]{0,1:T(8,128)(2,1)S(1)}, u32[]{:S(2)}, u32[]{:S(2)}) collective-permute-start(bf16[128,576]{0,1:T(8,128)(2,1)S(1)} %get-tuple-element.135), channel_id=1, source_target_pairs={{0,24},{1,25},{2,26},{3,27},{4,28},{5,29},{6,30},{7,31},{8,16},{9,... | collective-permute-start | bytes 442376 | tf_op jit(solution)/shard_map/ppermute | solution.py:23
  285.5 11.1 %collective-permute-start.24 = (bf16[128,576]{0,1:T(8,128)(2,1)S(1)}, bf16[128,576]{0,1:T(8,128)(2,1)S(1)}, u32[]{:S(2)}, u32[]{:S(2)}) collective-permute-start(bf16[128,576]{0,1:T(8,128)(2,1)S(1)} %get-tuple-element.136), channel_id=1, source_target_pairs={{0,16},{1,17},{2,18},{3,19},{4,20},{5,21},{6,22},{7,23},{8,24},{9,... | collective-permute-start | bytes 442376 | tf_op jit(solution)/shard_map/ppermute | solution.py:23
  288.4 11.7 %collective-permute-start.25 = (bf16[128,576]{0,1:T(8,128)(2,1)S(1)}, bf16[128,576]{0,1:T(8,128)(2,1)S(1)}, u32[]{:S(2)}, u32[]{:S(2)}) collective-permute-start(bf16[128,576]{0,1:T(8,128)(2,1)S(1)} %get-tuple-element.134), channel_id=1, source_target_pairs={{0,8},{1,9},{2,10},{3,11},{4,12},{5,13},{6,14},{7,15},{8,0},{9,1},... | collective-permute-start | bytes 442376 | tf_op jit(solution)/shard_map/ppermute | solution.py:23
  (78 other events, 814.1 us)
Sparse Core Ops, SparseCore 0:
  55.1 57.7 all-gather.1
